TPU v7x, 32 devices: a whole 2x2x4 slice. The times are simulated.
32 devices in a mesh: groups: 2 (over y), shard: 16 (over z, x, core).
Axes of the slice: x: 2, y: 2, z: 4, core: 2. Of those that a mesh axis runs over, the one named last changes fastest.
Arguments:
- traces: float32 [20736, 2048], P(('groups', 'shard')), parts along dimension 0, may hold values from -250 to 250
- cable_depth: float32 [32], P(('groups', 'shard')), parts along dimension 0, may hold values from 6 to 25
- receiver: int32 [20736], P(('groups', 'shard')), parts along dimension 0, may hold values from 0 to 671, as said below
- shot_slot: int32 [32], P('groups'), parts along dimension 0, may hold values from 0 to 15, as said below
- gather_home: int32 [1344], P('groups'), parts along dimension 0, may hold values from 0 to 671, each once
Outputs:
- filtered_gathers: float32 [1344, 16, 2048], P(('groups', 'shard')), parts along dimension 0
There are 2 independent parts, one for each index of `groups`. A program takes and returns all parts, laid end to end along the dimension named above; each array names one. Nothing has to cross between parts.
Inputs may be any that keep to these rules, and one draw needn't show every extreme that they name: The 648 receiver bins of one record are distinct. `shot_slot`: every record has a position of its own.
All inputs are finite; a program needn't handle non-finite values.
Results may differ from a plain program's by a relative error of at most 0.0081.
Values may be sent and summed in bfloat16 or wider, within the bound.
A program may use at most 64 MiB of HBM per device.

v0:
```python
import functools
import math

import jax
import jax.numpy as jnp
import ml_dtypes
import numpy as np
from jax import lax
from jax.experimental import pallas as pl
from jax.experimental.pallas import tpu as pltpu
from jax.sharding import PartitionSpec as P

FREQ = 576


sample_step = 0.002
water_speed = 1500.0
channel_spacing = 12.5
shot_spacing = 25.0
surface_reflect = 0.9
ghost_floor = 0.1
reject_speed = 1500.0
low_floor = 4.0 * math.pi
energy_eps = 1e-06


def forward_time(n_samples, first_bin, band_size):
    samples = jnp.arange(n_samples, dtype=jnp.int32)
    freq_bins = first_bin + jnp.arange(band_size, dtype=jnp.int32)
    angles = (samples[:, None] * freq_bins[None, :] % n_samples).astype(jnp.float32) * (
        2.0 * math.pi / n_samples
    )
    return jnp.concatenate([jnp.cos(angles), -jnp.sin(angles)], axis=1).astype(jnp.bfloat16)


def inverse_time(n_samples, first_bin, band_size):
    samples = jnp.arange(n_samples, dtype=jnp.int32)
    freq_bins = first_bin + jnp.arange(band_size, dtype=jnp.int32)
    angles = (freq_bins[:, None] * samples[None, :] % n_samples).astype(jnp.float32) * (
        2.0 * math.pi / n_samples
    )
    weights = jnp.where(freq_bins == 0, 1.0, 2.0).astype(jnp.float32)[:, None]
    return jnp.concatenate([weights * jnp.cos(angles), -weights * jnp.sin(angles)], axis=0).astype(
        jnp.bfloat16
    )


def wave_tables(n_channels):
    wave_index = jnp.arange(n_channels, dtype=jnp.int32)
    angles = (wave_index[:, None] * wave_index[None, :] % n_channels).astype(jnp.float32) * (
        2.0 * math.pi / n_channels
    )
    return (jnp.cos(angles).astype(jnp.bfloat16), jnp.sin(angles).astype(jnp.bfloat16))


def angular_band(n_samples, first_bin, band_size):
    freq_bins = (first_bin + jnp.arange(band_size, dtype=jnp.int32)).astype(jnp.float32)
    return 2.0 * math.pi * freq_bins / (n_samples * sample_step)


def ghost_operator(n_channels, n_samples, first_bin, band_size, depth_value):
    angular = angular_band(n_samples, first_bin, band_size)
    wave_index = jnp.arange(n_channels, dtype=jnp.int32)
    signed = jnp.where(wave_index <= n_channels // 2, wave_index, wave_index - n_channels).astype(
        jnp.float32
    )
    wave_number = 2.0 * math.pi * signed / (n_channels * channel_spacing)
    slowness = angular / water_speed
    vertical = jnp.sqrt(
        jnp.maximum(
            slowness[None, :] * slowness[None, :] - wave_number[:, None] * wave_number[:, None], 0.0
        )
    )
    angles = 2.0 * vertical * depth_value
    cosine = jnp.cos(angles)
    denominator = (
        1.0 - 2.0 * surface_reflect * cosine + surface_reflect * surface_reflect + ghost_floor
    )
    return (
        (1.0 - surface_reflect * cosine) / denominator,
        -surface_reflect * jnp.sin(angles) / denominator,
    )


def deghost(record, depth_value, first_bin, band_size):
    n_channels, n_samples = record.shape
    spectra = jnp.dot(
        record.astype(jnp.bfloat16),
        forward_time(n_samples, first_bin, band_size),
        preferred_element_type=jnp.float32,
    ).astype(jnp.bfloat16)
    cos_wave, sin_wave = wave_tables(n_channels)
    plain = jnp.dot(cos_wave, spectra, preferred_element_type=jnp.float32)
    turned = jnp.dot(sin_wave, spectra, preferred_element_type=jnp.float32)
    wave_re = plain[:, :band_size] + turned[:, band_size:]
    wave_im = plain[:, band_size:] - turned[:, :band_size]
    gain_re, gain_im = ghost_operator(n_channels, n_samples, first_bin, band_size, depth_value)
    lifted = jnp.concatenate(
        [gain_re * wave_re - gain_im * wave_im, gain_re * wave_im + gain_im * wave_re], axis=1
    ).astype(jnp.bfloat16)
    plain = jnp.dot(cos_wave, lifted, preferred_element_type=jnp.float32)
    turned = jnp.dot(sin_wave, lifted, preferred_element_type=jnp.float32)
    back_re = (plain[:, :band_size] - turned[:, band_size:]) / n_channels
    back_im = (plain[:, band_size:] + turned[:, :band_size]) / n_channels
    cleaned = jnp.concatenate([back_re, back_im], axis=1)
    return (cleaned.astype(jnp.bfloat16), jnp.sum(cleaned * cleaned))


def shot_tables(positions, records):
    wave_index = jnp.arange(2 * records, dtype=jnp.int32)
    angles = (positions[:, None] * wave_index[None, :] % (2 * records)).astype(jnp.float32) * (
        math.pi / records
    )
    return (jnp.cos(angles).astype(jnp.bfloat16), jnp.sin(angles).astype(jnp.bfloat16))


def shot_filter(records, n_samples, first_bin, band_size):
    angular = angular_band(n_samples, first_bin, band_size)
    wave_index = jnp.arange(2 * records, dtype=jnp.int32)
    signed = jnp.where(wave_index <= records, wave_index, wave_index - 2 * records).astype(
        jnp.float32
    )
    shot_number = 2.0 * math.pi * signed / (2 * records * shot_spacing)
    reject_ratio = reject_speed * jnp.abs(shot_number)[:, None] / (angular[None, :] + low_floor)
    squared = reject_ratio * reject_ratio
    response = 1.0 / (1.0 + squared * squared) / (2.0 * records)
    return jnp.concatenate([response, response], axis=1)


def place_rows(clean_rows, receiver, gather_home, records, per_device):
    targets = jnp.take(gather_home, receiver, axis=0)
    buffer = (
        jnp.zeros((records * per_device, clean_rows.shape[1]), jnp.bfloat16)
        .at[targets]
        .set(clean_rows)
    )
    return buffer.reshape(records, per_device, clean_rows.shape[1])


def filter_gathers(arrived, shot_slot, n_samples, first_bin, band_size):
    records = arrived.shape[0]
    cos_source, sin_source = shot_tables(shot_slot, records)
    cos_shot, sin_shot = shot_tables(jnp.arange(records, dtype=jnp.int32), records)
    response = shot_filter(records, n_samples, first_bin, band_size)[:, None, :]
    even_part = (
        jnp.einsum("sgf,sk->kgf", arrived, cos_source, preferred_element_type=jnp.float32)
        * response
    ).astype(jnp.bfloat16)
    odd_part = (
        jnp.einsum("sgf,sk->kgf", arrived, sin_source, preferred_element_type=jnp.float32)
        * response
    ).astype(jnp.bfloat16)
    filtered = (
        jnp.einsum("pk,kgf->gpf", cos_shot, even_part, preferred_element_type=jnp.float32)
        + jnp.einsum("pk,kgf->gpf", sin_shot, odd_part, preferred_element_type=jnp.float32)
    ).astype(jnp.bfloat16)
    return jnp.einsum(
        "gpf,ft->gpt",
        filtered,
        inverse_time(n_samples, first_bin, band_size),
        preferred_element_type=jnp.float32,
    )


def shards(traces, cable_depth, receiver, shot_slot, gather_home):
    records = lax.axis_size("shard")
    per_device = gather_home.shape[0] // records
    n_channels, n_samples = traces.shape
    clean_rows, energy = deghost(traces, cable_depth[0], 0, FREQ)
    outgoing = place_rows(clean_rows, receiver, gather_home, records, per_device)
    arrived = lax.all_to_all(outgoing, "shard", split_axis=0, concat_axis=0, tiled=True)
    summed = filter_gathers(arrived, shot_slot, n_samples, 0, FREQ)
    total_energy = lax.psum(energy, "shard")
    out_scale = 1.0 / jnp.sqrt(
        2.0 * FREQ * (total_energy / (n_channels * records * FREQ) + energy_eps)
    )
    return summed * out_scale


def round_up(value, unit):
    return -(-value // unit) * unit


LANES = 128
HALF = LANES // 2
GROUP = 3


def fused_tables(n_channels, n_samples, records, per_device):
    bf16 = ml_dtypes.bfloat16
    blocks = FREQ // HALF
    bins = np.arange(FREQ).reshape(blocks, HALF)
    samples = np.arange(n_samples)
    turn = 2.0 * np.pi / n_samples
    angle = (samples[:, None] * np.arange(FREQ)[None, :] % n_samples) * turn
    cos_t = np.cos(angle).reshape(n_samples, blocks, 1, HALF)
    sin_t = np.sin(angle).reshape(n_samples, blocks, 1, HALF)
    forward = np.concatenate([cos_t, -sin_t], axis=2).reshape(n_samples, blocks * LANES)
    weight = np.where(bins == 0, 1.0, 2.0)[None, :, None, :]
    inverse = np.concatenate([weight * cos_t, -weight * sin_t], axis=2)
    inverse = inverse.reshape(n_samples, blocks * LANES).T
    chunks = blocks // GROUP
    forward = forward.reshape(n_samples, chunks, GROUP * LANES).transpose(1, 0, 2)

    half_rows = round_up(n_channels // 2 + 1, 16)
    wave = np.zeros((2 * half_rows, 2 * half_rows))
    index = np.arange(n_channels // 2 + 1)
    angle = (index[:, None] * np.arange(n_channels)[None, :] % n_channels) * (
        2.0 * np.pi / n_channels
    )
    wave[: index.size, :n_channels] = np.cos(angle)
    wave[half_rows : half_rows + index.size, :n_channels] = np.sin(angle)
    own_mirror = (index * 2) % n_channels == 0
    wave[half_rows : half_rows + index.size][own_mirror] = 0.0
    twice = np.ones((2 * half_rows, 1))
    twice[: index.size, 0] = np.where(own_mirror, 1.0, 2.0)
    twice[half_rows : half_rows + index.size, 0] = 2.0
    wave = wave.astype(bf16)
    back = (wave.astype(np.float64) * twice).T.astype(bf16)

    angular = 2.0 * np.pi * np.arange(FREQ) / (n_samples * sample_step)
    number = 2.0 * np.pi * np.arange(half_rows) / (n_channels * channel_spacing)
    vertical = np.sqrt(
        np.maximum((angular / water_speed)[None, :] ** 2 - number[:, None] ** 2, 0.0)
    )
    vertical = (vertical / np.pi).reshape(half_rows, blocks, 1, HALF)
    vertical = np.concatenate([vertical, vertical], axis=2).reshape(half_rows, blocks * LANES)

    shots = np.arange(2 * records)
    signed = np.where(shots <= records, shots, shots - 2 * records)
    shot_number = 2.0 * np.pi * signed / (2 * records * shot_spacing)
    ratio = reject_speed * np.abs(shot_number)[:, None] / (angular[None, :] + low_floor)
    response = 1.0 / (1.0 + ratio**4) / (2.0 * records)
    apart = np.arange(records)
    lag = np.cos(np.pi / records * (apart[:, None] * shots[None, :] % (2 * records))) @ response
    lag = lag.reshape(records, chunks, GROUP, 1, HALF)
    lag = np.broadcast_to(lag, (records, chunks, GROUP, 2, HALF)).reshape(
        records, chunks, GROUP, 1, LANES
    )
    packed = round_up(GROUP * per_device, 16)
    taps = np.zeros((chunks, records, packed, LANES))
    taps[:, :, : GROUP * per_device] = (
        np.broadcast_to(lag, (records, chunks, GROUP, per_device, LANES))
        .transpose(1, 0, 2, 3, 4)
        .reshape(chunks, records, GROUP * per_device, LANES)
    )
    return (
        forward.astype(bf16),
        inverse.astype(bf16),
        wave,
        back,
        vertical.astype(np.float32),
        taps.astype(np.float32),
    )


SINE = [(-1.0) ** i * (2.0 * math.pi) ** (2 * i + 1) / math.factorial(2 * i + 1) for i in range(6)]


def gain_tiles(vertical, depth, n_channels):
    left = lax.broadcasted_iota(jnp.int32, vertical.shape, 1) < HALF
    turns = vertical * depth - jnp.where(left, 0.25, 0.0)
    offset = 0.25 - jnp.abs(turns - jnp.floor(turns + 0.5))
    square = offset * offset
    value = jnp.full_like(square, SINE[-1])
    for coefficient in SINE[-2::-1]:
        value = value * square + coefficient
    value = value * offset
    swapped = pltpu.roll(value, HALF, 1)
    cosine = jnp.where(left, swapped, value)
    sine = jnp.where(left, value, -swapped)
    denominator = (
        1.0 - 2.0 * surface_reflect * cosine + surface_reflect * surface_reflect + ghost_floor
    )
    scale = 1.0 / (denominator * n_channels)
    return (1.0 - surface_reflect * cosine) * scale, surface_reflect * sine * scale


def exchange_kernel(
    records,
    per_device,
    chunks,
    traces,
    forward,
    wave,
    back,
    vertical,
    taps,
    depth,
    order,
    home,
    receiver,
    filtered,
    energy,
    raw,
    rounded,
    table,
    lag,
    placed,
    spectra,
    lifted,
    packed,
    shots,
    ordered,
    sums,
    load_sem,
    send_sem,
    recv_sem,
    sum_send,
    sum_recv,
    *slots,
):
    outgoing, arrived = slots[:chunks], slots[chunks:]
    me = lax.axis_index("shard")
    n_channels, n_samples = raw.shape
    padded = rounded.shape[0]
    half_rows = padded // 2
    home_rows = placed.shape[0]
    stride = home_rows // records

    def partner(step):
        if records & (records - 1):
            return lax.rem(me + step, records)
        other = me
        bit = 1
        while bit < records:
            if step & bit:
                other = other + bit * (1 - 2 * lax.rem(me // bit, 2))
            bit *= 2
        return other

    steps = [s for s in range(records - 1, 0, -1)]

    copies = [pltpu.make_async_copy(traces, raw, load_sem.at[0])]
    for c in range(chunks):
        copies.append(pltpu.make_async_copy(forward.at[c], table.at[c], load_sem.at[1 + 2 * c]))
        copies.append(pltpu.make_async_copy(taps.at[c], lag.at[c], load_sem.at[2 + 2 * c]))
    for copy in copies[:2]:
        copy.start()

    barrier = pltpu.get_barrier_semaphore()
    for step in steps:
        pl.semaphore_signal(
            barrier,
            inc=1,
            device_id={"shard": partner(step)},
            device_id_type=pl.DeviceIdType.MESH,
        )

    bins = lax.broadcasted_iota(jnp.int32, (home.shape[1], padded), 0)
    chosen = (bins == receiver[...]).astype(jnp.bfloat16)
    by_bin = jnp.dot(chosen, back[...], preferred_element_type=jnp.float32).astype(jnp.bfloat16)
    rows = lax.broadcasted_iota(jnp.int32, (home_rows, home.shape[1]), 0)
    chosen = (rows == home[...]).astype(jnp.bfloat16)
    placed[...] = jnp.dot(chosen, by_bin, preferred_element_type=jnp.float32).astype(jnp.bfloat16)
    packed[...] = jnp.zeros_like(packed)
    rounded[...] = jnp.zeros_like(rounded)

    copies[0].wait()
    for copy in copies[2:]:
        copy.start()
    rounded[:n_channels, :] = raw[...].astype(jnp.bfloat16)

    total = jnp.zeros((8, LANES), jnp.float32)
    sends = []
    for c in range(chunks):
        copies[1 + 2 * c].wait()
        spectra[...] = jnp.dot(
            rounded[...], table[c], preferred_element_type=jnp.float32
        ).astype(jnp.bfloat16)
        turned = jnp.dot(wave[...], spectra[...], preferred_element_type=jnp.float32)
        for b in range(GROUP):
            lanes = slice(b * LANES, (b + 1) * LANES)
            column = c * GROUP + b
            straight, crossed = gain_tiles(
                vertical[:, column * LANES : (column + 1) * LANES], depth[0], n_channels
            )
            for part in range(2):
                part_rows = slice(part * half_rows, (part + 1) * half_rows)
                value = turned[part_rows, lanes]
                lifted[part_rows, lanes] = (
                    straight * value + crossed * pltpu.roll(value, HALF, 1)
                ).astype(jnp.bfloat16)
        cleaned = jnp.dot(placed[...], lifted[...], preferred_element_type=jnp.float32)
        for b in range(GROUP):
            block = cleaned[:, b * LANES : (b + 1) * LANES]
            total = total + jnp.sum((block * block).reshape(-1, 8, LANES), axis=0)
            for d in range(records):
                packed[d, b * per_device : (b + 1) * per_device, :] = block[
                    d * stride : d * stride + per_device
                ]
        outgoing[c][...] = packed[...].astype(jnp.bfloat16)
        if c == 0:
            pl.semaphore_wait(barrier, records - 1)
        for i, step in enumerate(steps):
            other = partner(step)
            send = pltpu.make_async_remote_copy(
                src_ref=outgoing[c].at[other],
                dst_ref=arrived[c].at[me],
                send_sem=send_sem.at[c, i],
                recv_sem=recv_sem.at[c, i],
                device_id={"shard": other},
                device_id_type=pl.DeviceIdType.MESH,
            )
            send.start()
            sends.append(send)
        arrived[c][me] = outgoing[c][me]

    sums[me] = total
    for i, step in enumerate(steps):
        send = pltpu.make_async_remote_copy(
            src_ref=sums.at[me],
            dst_ref=sums.at[me],
            send_sem=sum_send.at[i],
            recv_sem=sum_recv.at[i],
            device_id={"shard": partner(step)},
            device_id_type=pl.DeviceIdType.MESH,
        )
        send.start()
        sends.append(send)

    tile = 16
    for c in range(chunks):
        copies[2 + 2 * c].wait()
        for send in sends[c * len(steps) : (c + 1) * len(steps)]:
            send.wait()

        def filter_rows(r, carry):
            at = pl.ds(pl.multiple_of(r * tile, tile), tile)
            values = [arrived[c][order[q], at, :].astype(jnp.float32) for q in range(records)]
            for p in range(records):
                result = None
                for q in range(records):
                    term = lag[c, abs(p - q), at, :] * values[q]
                    result = term if result is None else result + term
                shots[p, at, :] = result
            return carry

        lax.fori_loop(0, shots.shape[1] // tile, filter_rows, 0)
        for b in range(GROUP):
            for p in range(records):
                ordered[b, pl.ds(p, per_device, stride=records), :] = shots[
                    p, b * per_device : (b + 1) * per_device, :
                ]
            column = c * GROUP + b
            filtered[:, column * LANES : (column + 1) * LANES] = ordered[b].astype(jnp.bfloat16)
    for send in sends[chunks * len(steps) :]:
        send.wait()
    energy[...] = jnp.sum(sums[...], axis=0)


def exchange(traces, cable_depth, receiver, shot_slot, gather_home, tables, records):
    forward, _, wave, back, vertical, taps = tables
    n_channels, n_samples = traces.shape
    n_bins = gather_home.shape[0]
    per_device = n_bins // records
    chunks, _, packed_rows, _ = taps.shape
    stride = round_up(per_device, 16)
    padded = wave.shape[0]
    order = jnp.sum(
        jnp.where(
            shot_slot[None, :] == jnp.arange(records, dtype=jnp.int32)[:, None],
            jnp.arange(records, dtype=jnp.int32)[None, :],
            0,
        ),
        axis=1,
    )
    home = (gather_home // per_device * stride + gather_home % per_device)[None, :]
    channels = jnp.pad(receiver, (0, padded - n_channels), constant_values=-1)[None, :]
    vmem = pl.BlockSpec(memory_space=pltpu.VMEM)
    smem = pl.BlockSpec(memory_space=pltpu.SMEM)
    anywhere = pl.BlockSpec(memory_space=pl.ANY)
    width = GROUP * LANES
    peers = records - 1
    slot = pltpu.VMEM((records, packed_rows, LANES), jnp.bfloat16)
    return pl.pallas_call(
        functools.partial(exchange_kernel, records, per_device, chunks),
        out_shape=(
            jax.ShapeDtypeStruct((per_device * records, chunks * width), jnp.bfloat16),
            jax.ShapeDtypeStruct((8, LANES), jnp.float32),
        ),
        in_specs=[anywhere, anywhere, vmem, vmem, vmem, anywhere, smem, smem, vmem, vmem],
        out_specs=(vmem, vmem),
        scratch_shapes=[
            pltpu.VMEM((n_channels, n_samples), jnp.float32),
            pltpu.VMEM((padded, n_samples), jnp.bfloat16),
            pltpu.VMEM(forward.shape, jnp.bfloat16),
            pltpu.VMEM(taps.shape, jnp.float32),
            pltpu.VMEM((records * stride, padded), jnp.bfloat16),
            pltpu.VMEM((padded, width), jnp.bfloat16),
            pltpu.VMEM((padded, width), jnp.bfloat16),
            pltpu.VMEM((records, packed_rows, LANES), jnp.float32),
            pltpu.VMEM((records, packed_rows, LANES), jnp.float32),
            pltpu.VMEM((GROUP, per_device * records, LANES), jnp.float32),
            pltpu.VMEM((records, 8, LANES), jnp.float32),
            pltpu.SemaphoreType.DMA((1 + 2 * chunks,)),
            pltpu.SemaphoreType.DMA((chunks, peers)),
            pltpu.SemaphoreType.DMA((chunks, peers)),
            pltpu.SemaphoreType.DMA((peers,)),
            pltpu.SemaphoreType.DMA((peers,)),
        ]
        + [slot] * (2 * chunks),
        compiler_params=pltpu.CompilerParams(
            collective_id=0, has_side_effects=True, vmem_limit_bytes=56 * 1024 * 1024
        ),
    )(traces, forward, wave, back, vertical, taps, cable_depth, order, home, channels)


def inverse_kernel(count, energy, filtered, inverse, out):
    total = jnp.sum(energy[...])
    scale = lax.rsqrt(jnp.full((1, 1), 2.0 * FREQ, jnp.float32) * (total / count + energy_eps))
    out[...] = (
        jnp.dot(filtered[...], inverse[...], preferred_element_type=jnp.float32) * scale
    )


def invert(filtered, energy, inverse, count):
    n_rows, depth = filtered.shape
    n_samples = inverse.shape[1]
    block = 512
    return pl.pallas_call(
        functools.partial(inverse_kernel, count),
        out_shape=jax.ShapeDtypeStruct((n_rows, n_samples), jnp.float32),
        grid=(n_samples // block,),
        in_specs=[
            pl.BlockSpec((8, LANES), lambda i: (0, 0)),
            pl.BlockSpec((n_rows, depth), lambda i: (0, 0)),
            pl.BlockSpec((depth, block), lambda i: (0, i)),
        ],
        out_specs=pl.BlockSpec((n_rows, block), lambda i: (0, i)),
        compiler_params=pltpu.CompilerParams(vmem_limit_bytes=48 * 1024 * 1024),
    )(energy, filtered, inverse)


def fused_shards(traces, cable_depth, receiver, shot_slot, gather_home):
    records = lax.axis_size("shard")
    n_channels, n_samples = traces.shape
    per_device = gather_home.shape[0] // records
    tables = fused_tables(n_channels, n_samples, records, per_device)
    filtered, energy = exchange(
        traces, cable_depth, receiver, shot_slot, gather_home, tables, records
    )
    out = invert(filtered, energy, tables[1], float(n_channels * records * FREQ))
    return out.reshape(per_device, records, n_samples)


def solution(mesh):
    in_specs = (
        P(("groups", "shard"), None),
        P(("groups", "shard")),
        P(("groups", "shard")),
        P("groups"),
        P("groups"),
    )
    out_specs = P(("groups", "shard"), None, None)
    body = fused_shards if mesh.shape["shard"] <= 16 else shards
    return jax.shard_map(body, mesh=mesh, in_specs=in_specs, out_specs=out_specs, check_vma=False)
```

profile of v0, /device:TPU:0, one launch (start us, length us, event | category | flops | bytes accessed | tf_op | source)
XLA Modules:
  0.0 66.0 jit_solution(2137757027982588194)
XLA Ops:
  0.7 1.3 %select_reduce_fusion.order = s32[16]{0:T(128)} fusion(s32[16]{0:T(128)} %param.14), kind=kLoop, calls=%fused_computation | loop fusion | flops 752 | bytes 128 | tf_op jit(solution)/shard_map/reduce_sum | solution.py:460
  2.0 0.7 %pad.4 = s32[672]{0:T(1024)S(1)} pad(s32[648]{0:T(1024)} %param.13, s32[]{:T(128)} %constant.34.clone.1), padding=0_24 | pad | bytes 5284 | tf_op jit(solution)/shard_map/jit(_pad)/pad | solution.py:469
  2.6 0.6 broadcast_in_dim.24.receiver
  3.2 0.7 %fusion.1 = s32[672]{0:T(1024)S(1)} fusion(s32[672]{0:T(1024)} %param.15), kind=kLoop, calls=%fused_computation.5 | loop fusion | flops 9408 | bytes 5376 | tf_op jit(solution)/shard_map/add | solution.py:468
  3.9 0.6 broadcast_in_dim.23.home
  4.5 52.0 %shard_map.109 = (bf16[672,1152]{1,0:T(8,128)(2,1)}, f32[8,128]{1,0:T(8,128)}) custom-call(f32[648,2048]{1,0:T(8,128)} %traces.1, bf16[3,2048,384]{2,1,0:T(8,128)(2,1)} %constant.36.clone.forward, bf16[672,672]{1,0:T(8,128)(2,1)} %constant.37.clone.wave, bf16[672,672]{1,0:T(8,128)(2,1)} %constant.38.clone.back, f32[336,1152]{1,0:T(8,128)} %constant.39.clone.vertical, ...), custom_call_target="tpu_custom_call" | custom-call | tf_op jit(solution)/shard_map/pallas_call | solution.py:476
  56.5 0.0 copy-start
  56.5 1.4 %copy-done = bf16[672,1152]{1,0:T(8,128)(2,1)S(1)} copy-done((bf16[672,1152]{1,0:T(8,128)(2,1)S(1)}, bf16[672,1152]{1,0:T(8,128)(2,1)}, u32[]{:S(2)}) %copy-start) | copy-done | bytes 1548312
  57.9 0.0 copy-start.1
  57.9 0.7 %copy-done.1 = f32[8,128]{1,0:T(8,128)S(1)} copy-done((f32[8,128]{1,0:T(8,128)S(1)}, f32[8,128]{1,0:T(8,128)}, u32[]{:S(2)}) %copy-start.1) | copy-done | bytes 4120
  58.6 7.4 %shard_map.110 = f32[672,2048]{1,0:T(8,128)} custom-call(f32[8,128]{1,0:T(8,128)S(1)} %copy-done.1, bf16[672,1152]{1,0:T(8,128)(2,1)S(1)} %copy-done, bf16[1152,2048]{1,0:T(8,128)(2,1)} %constant.41.clone.inverse), custom_call_target="tpu_custom_call" | custom-call | tf_op jit(solution)/shard_map/pallas_call | solution.py:521
Async XLA Ops:
  56.5 1.4 %copy-start = (bf16[672,1152]{1,0:T(8,128)(2,1)S(1)}, bf16[672,1152]{1,0:T(8,128)(2,1)}, u32[]{:S(2)}) copy-start(bf16[672,1152]{1,0:T(8,128)(2,1)} %get-tuple-element.8.filtered) | copy-start | bytes 4644868
  57.9 0.7 %copy-start.1 = (f32[8,128]{1,0:T(8,128)S(1)}, f32[8,128]{1,0:T(8,128)}, u32[]{:S(2)}) copy-start(f32[8,128]{1,0:T(8,128)} %get-tuple-element.7.energy) | copy-start | bytes 12292
where the time goes:
time: 66.4 us; the launch traced here: 66 us
  Pallas kernels  59.4 us (89%)
  local copies, waits for them, and re-layouts  3.92 us (6%)
  other arithmetic  2.01 us (3%)
  between operations  0.67 us (1%)
    pallas_call x1, Pallas kernels, exchange(): pl.pallas_call(functools.partial(exchange_kernel, records, per_device, ch...  52 us
    pallas_call x1, Pallas kernels, invert(): pl.pallas_call(functools.partial(inverse_kernel, count), out_shape=jax.Sh...  7.42 us
    unnamed x4, local copies, waits for them, and re-layouts  2.07 us

commit v1 on v0

--- a/solution.py
+++ b/solution.py
@@ -183,7 +183,7 @@
 
 LANES = 128
 HALF = LANES // 2
-GROUP = 3
+GROUPS = (1, 3, 3, 2)
 
 
 def fused_tables(n_channels, n_samples, records, per_device):
@@ -199,9 +199,6 @@
     weight = np.where(bins == 0, 1.0, 2.0)[None, :, None, :]
     inverse = np.concatenate([weight * cos_t, -weight * sin_t], axis=2)
     inverse = inverse.reshape(n_samples, blocks * LANES).T
-    chunks = blocks // GROUP
-    forward = forward.reshape(n_samples, chunks, GROUP * LANES).transpose(1, 0, 2)
-
     half_rows = round_up(n_channels // 2 + 1, 16)
     wave = np.zeros((2 * half_rows, 2 * half_rows))
     index = np.arange(n_channels // 2 + 1)
@@ -233,17 +230,18 @@
     response = 1.0 / (1.0 + ratio**4) / (2.0 * records)
     apart = np.arange(records)
     lag = np.cos(np.pi / records * (apart[:, None] * shots[None, :] % (2 * records))) @ response
-    lag = lag.reshape(records, chunks, GROUP, 1, HALF)
-    lag = np.broadcast_to(lag, (records, chunks, GROUP, 2, HALF)).reshape(
-        records, chunks, GROUP, 1, LANES
-    )
-    packed = round_up(GROUP * per_device, 16)
-    taps = np.zeros((chunks, records, packed, LANES))
-    taps[:, :, : GROUP * per_device] = (
-        np.broadcast_to(lag, (records, chunks, GROUP, per_device, LANES))
-        .transpose(1, 0, 2, 3, 4)
-        .reshape(chunks, records, GROUP * per_device, LANES)
-    )
+    lag = lag.reshape(records, blocks, 1, HALF)
+    lag = np.concatenate([lag, lag], axis=2).reshape(records, blocks, 1, LANES)
+    lag = np.broadcast_to(lag, (records, blocks, per_device, LANES))
+    taps = []
+    first = 0
+    for group in GROUPS:
+        filled = group * per_device
+        part = np.zeros((records, round_up(filled, 16), LANES))
+        part[:, :filled] = lag[:, first : first + group].reshape(records, filled, LANES)
+        taps.append(part)
+        first += group
+    taps = np.concatenate(taps, axis=1)
     return (
         forward.astype(bf16),
         inverse.astype(bf16),
@@ -279,29 +277,37 @@
 def exchange_kernel(
     records,
     per_device,
-    chunks,
+    stride,
     traces,
     forward,
+    wave_table,
+    back_table,
+    vertical_table,
+    taps,
+    inverse_table,
+    depth,
+    shot_slot,
+    home,
+    receiver,
+    last,
+    energy,
+    partial,
+    raw,
+    rounded,
+    table,
     wave,
     back,
     vertical,
-    taps,
-    depth,
-    order,
-    home,
-    receiver,
-    filtered,
-    energy,
-    raw,
-    rounded,
-    table,
     lag,
+    inverse,
     placed,
     spectra,
     lifted,
     packed,
     shots,
     ordered,
+    filtered,
+    summed,
     sums,
     load_sem,
     send_sem,
@@ -310,36 +316,57 @@
     sum_recv,
     *slots,
 ):
+    chunks = len(GROUPS)
     outgoing, arrived = slots[:chunks], slots[chunks:]
     me = lax.axis_index("shard")
     n_channels, n_samples = raw.shape
     padded = rounded.shape[0]
     half_rows = padded // 2
     home_rows = placed.shape[0]
-    stride = home_rows // records
+    peers = records - 1
+    firsts = [sum(GROUPS[:c]) for c in range(chunks + 1)]
+    packed_rows = [ref.shape[1] for ref in outgoing]
+    tap_rows = [sum(packed_rows[:c]) for c in range(chunks)]
+
+    start = (lax.rem(me // 4, 2) * 2 + lax.rem(me, 2)) * peers // 4
+
+    def turn(i):
+        return peers - lax.rem(start + i, peers)
 
     def partner(step):
         if records & (records - 1):
             return lax.rem(me + step, records)
-        other = me
+        other = 0
         bit = 1
         while bit < records:
-            if step & bit:
-                other = other + bit * (1 - 2 * lax.rem(me // bit, 2))
+            other = other + bit * lax.rem(me // bit + step // bit, 2)
             bit *= 2
         return other
 
-    steps = [s for s in range(records - 1, 0, -1)]
-
-    copies = [pltpu.make_async_copy(traces, raw, load_sem.at[0])]
-    for c in range(chunks):
-        copies.append(pltpu.make_async_copy(forward.at[c], table.at[c], load_sem.at[1 + 2 * c]))
-        copies.append(pltpu.make_async_copy(taps.at[c], lag.at[c], load_sem.at[2 + 2 * c]))
-    for copy in copies[:2]:
+    sem_count = [0]
+
+    def load(source, target):
+        copy = pltpu.make_async_copy(source, target, load_sem.at[sem_count[0]])
+        sem_count[0] += 1
         copy.start()
+        return copy
+
+    def load_columns(c):
+        lanes = pl.ds(firsts[c] * LANES, GROUPS[c] * LANES)
+        return load(forward.at[:, lanes], table.at[:, lanes])
+
+    piece = round_up(-(-n_channels // 3), 16)
+    back_load = load(back_table, back)
+    pieces = []
+    for row in range(0, n_channels, piece):
+        rows = pl.ds(row, min(piece, n_channels - row))
+        pieces.append((row, load(traces.at[rows, :], raw.at[rows, :])))
+    column_loads = [load_columns(0)]
+    wave_load = load(wave_table, wave)
+    vertical_load = load(vertical_table, vertical)
 
     barrier = pltpu.get_barrier_semaphore()
-    for step in steps:
+    for step in range(1, records):
         pl.semaphore_signal(
             barrier,
             inc=1,
@@ -347,31 +374,48 @@
             device_id_type=pl.DeviceIdType.MESH,
         )
 
-    bins = lax.broadcasted_iota(jnp.int32, (home.shape[1], padded), 0)
-    chosen = (bins == receiver[...]).astype(jnp.bfloat16)
+    packed[...] = jnp.zeros_like(packed)
+    rounded[n_channels // 16 * 16 :, :] = jnp.zeros_like(rounded[n_channels // 16 * 16 :, :])
+    n_bins = home.shape[0]
+    homes = home[...].reshape(1, n_bins)
+    moved = homes
+    for d in range(1, records):
+        moved = moved + jnp.where(homes >= d * per_device, stride - per_device, 0)
+    bins = lax.broadcasted_iota(jnp.int32, (n_bins, n_channels), 0)
+    chosen = (bins == receiver[...].reshape(1, n_channels)).astype(jnp.bfloat16)
+    back_load.wait()
     by_bin = jnp.dot(chosen, back[...], preferred_element_type=jnp.float32).astype(jnp.bfloat16)
-    rows = lax.broadcasted_iota(jnp.int32, (home_rows, home.shape[1]), 0)
-    chosen = (rows == home[...]).astype(jnp.bfloat16)
+    rows = lax.broadcasted_iota(jnp.int32, (home_rows, n_bins), 0)
+    chosen = (rows == moved).astype(jnp.bfloat16)
     placed[...] = jnp.dot(chosen, by_bin, preferred_element_type=jnp.float32).astype(jnp.bfloat16)
-    packed[...] = jnp.zeros_like(packed)
-    rounded[...] = jnp.zeros_like(rounded)
-
-    copies[0].wait()
-    for copy in copies[2:]:
-        copy.start()
-    rounded[:n_channels, :] = raw[...].astype(jnp.bfloat16)
+
+    for row, copy in pieces:
+        copy.wait()
+        end = min(row + piece, n_channels)
+        rounded[row:end, :] = raw[row:end, :].astype(jnp.bfloat16)
+    column_loads += [load_columns(c) for c in range(1, chunks)]
+    lag_load = load(taps, lag)
+    inverse_load = load(inverse_table, inverse)
 
     total = jnp.zeros((8, LANES), jnp.float32)
     sends = []
-    for c in range(chunks):
-        copies[1 + 2 * c].wait()
-        spectra[...] = jnp.dot(
-            rounded[...], table[c], preferred_element_type=jnp.float32
+    for c, group in enumerate(GROUPS):
+        column_loads[c].wait()
+        spectra[:, : group * LANES] = jnp.dot(
+            rounded[...],
+            table[:, firsts[c] * LANES : firsts[c + 1] * LANES],
+            preferred_element_type=jnp.float32,
         ).astype(jnp.bfloat16)
-        turned = jnp.dot(wave[...], spectra[...], preferred_element_type=jnp.float32)
-        for b in range(GROUP):
+        if c == 0:
+            wave_load.wait()
+        turned = jnp.dot(
+            wave[...], spectra[:, : group * LANES], preferred_element_type=jnp.float32
+        )
+        if c == 0:
+            vertical_load.wait()
+        for b in range(group):
             lanes = slice(b * LANES, (b + 1) * LANES)
-            column = c * GROUP + b
+            column = firsts[c] + b
             straight, crossed = gain_tiles(
                 vertical[:, column * LANES : (column + 1) * LANES], depth[0], n_channels
             )
@@ -381,24 +425,27 @@
                 lifted[part_rows, lanes] = (
                     straight * value + crossed * pltpu.roll(value, HALF, 1)
                 ).astype(jnp.bfloat16)
-        cleaned = jnp.dot(placed[...], lifted[...], preferred_element_type=jnp.float32)
-        for b in range(GROUP):
+        cleaned = jnp.dot(
+            placed[...], lifted[:, : group * LANES], preferred_element_type=jnp.float32
+        )
+        for b in range(group):
             block = cleaned[:, b * LANES : (b + 1) * LANES]
             total = total + jnp.sum((block * block).reshape(-1, 8, LANES), axis=0)
             for d in range(records):
                 packed[d, b * per_device : (b + 1) * per_device, :] = block[
                     d * stride : d * stride + per_device
                 ]
-        outgoing[c][...] = packed[...].astype(jnp.bfloat16)
+        outgoing[c][...] = packed[:, : packed_rows[c], :].astype(jnp.bfloat16)
         if c == 0:
-            pl.semaphore_wait(barrier, records - 1)
-        for i, step in enumerate(steps):
+            pl.semaphore_wait(barrier, peers)
+        for i in range(peers):
+            step = turn(i)
             other = partner(step)
             send = pltpu.make_async_remote_copy(
                 src_ref=outgoing[c].at[other],
                 dst_ref=arrived[c].at[me],
-                send_sem=send_sem.at[c, i],
-                recv_sem=recv_sem.at[c, i],
+                send_sem=send_sem.at[c, step - 1],
+                recv_sem=recv_sem.at[c, step - 1],
                 device_id={"shard": other},
                 device_id_type=pl.DeviceIdType.MESH,
             )
@@ -407,129 +454,175 @@
         arrived[c][me] = outgoing[c][me]
 
     sums[me] = total
-    for i, step in enumerate(steps):
+    for i in range(peers):
+        step = turn(i)
         send = pltpu.make_async_remote_copy(
             src_ref=sums.at[me],
             dst_ref=sums.at[me],
-            send_sem=sum_send.at[i],
-            recv_sem=sum_recv.at[i],
+            send_sem=sum_send.at[step - 1],
+            recv_sem=sum_recv.at[step - 1],
             device_id={"shard": partner(step)},
             device_id_type=pl.DeviceIdType.MESH,
         )
         send.start()
         sends.append(send)
 
+    order = []
+    for q in range(records):
+        place = jnp.int32(0)
+        for s in range(records):
+            place = jnp.where(shot_slot[s] == q, s, place)
+        order.append(place)
+    lag_load.wait()
+    inverse_load.wait()
     tile = 16
-    for c in range(chunks):
-        copies[2 + 2 * c].wait()
-        for send in sends[c * len(steps) : (c + 1) * len(steps)]:
+    done = 0
+    for c, group in enumerate(GROUPS):
+        for send in sends[c * peers : (c + 1) * peers]:
             send.wait()
 
         def filter_rows(r, carry):
             at = pl.ds(pl.multiple_of(r * tile, tile), tile)
+            tap_at = pl.ds(pl.multiple_of(tap_rows[c] + r * tile, tile), tile)
             values = [arrived[c][order[q], at, :].astype(jnp.float32) for q in range(records)]
             for p in range(records):
                 result = None
                 for q in range(records):
-                    term = lag[c, abs(p - q), at, :] * values[q]
+                    term = lag[abs(p - q), tap_at, :] * values[q]
                     result = term if result is None else result + term
                 shots[p, at, :] = result
             return carry
 
-        lax.fori_loop(0, shots.shape[1] // tile, filter_rows, 0)
-        for b in range(GROUP):
+        lax.fori_loop(0, packed_rows[c] // tile, filter_rows, 0)
+        for b in range(group):
             for p in range(records):
                 ordered[b, pl.ds(p, per_device, stride=records), :] = shots[
                     p, b * per_device : (b + 1) * per_device, :
                 ]
-            column = c * GROUP + b
-            filtered[:, column * LANES : (column + 1) * LANES] = ordered[b].astype(jnp.bfloat16)
-    for send in sends[chunks * len(steps) :]:
+            if c == chunks - 1:
+                last[:, b * LANES : (b + 1) * LANES] = ordered[b].astype(jnp.bfloat16)
+            else:
+                column = firsts[c] + b
+                filtered[:, column * LANES : (column + 1) * LANES] = ordered[b].astype(
+                    jnp.bfloat16
+                )
+        if 0 < c < chunks - 1:
+            depth_at = slice(done * LANES, firsts[c + 1] * LANES)
+            for n in range(0, n_samples, 512):
+                part = jnp.dot(
+                    filtered[:, depth_at],
+                    inverse[depth_at, n : n + 512],
+                    preferred_element_type=jnp.float32,
+                )
+                if done:
+                    part = summed[:, n : n + 512] + part
+                summed[:, n : n + 512] = part
+            done = firsts[c + 1]
+        if c == chunks - 2:
+            store = pltpu.make_async_copy(summed, partial, load_sem.at[sem_count[0]])
+            store.start()
+    for send in sends[chunks * peers :]:
         send.wait()
     energy[...] = jnp.sum(sums[...], axis=0)
+    store.wait()
 
 
 def exchange(traces, cable_depth, receiver, shot_slot, gather_home, tables, records):
-    forward, _, wave, back, vertical, taps = tables
+    forward, inverse, wave, back, vertical, taps = tables
+    back = back[: traces.shape[0]]
     n_channels, n_samples = traces.shape
     n_bins = gather_home.shape[0]
     per_device = n_bins // records
-    chunks, _, packed_rows, _ = taps.shape
     stride = round_up(per_device, 16)
     padded = wave.shape[0]
-    order = jnp.sum(
-        jnp.where(
-            shot_slot[None, :] == jnp.arange(records, dtype=jnp.int32)[:, None],
-            jnp.arange(records, dtype=jnp.int32)[None, :],
-            0,
-        ),
-        axis=1,
-    )
-    home = (gather_home // per_device * stride + gather_home % per_device)[None, :]
-    channels = jnp.pad(receiver, (0, padded - n_channels), constant_values=-1)[None, :]
+    n_rows = per_device * records
+    chunks = len(GROUPS)
+    early = sum(GROUPS[:-1]) * LANES
     vmem = pl.BlockSpec(memory_space=pltpu.VMEM)
     smem = pl.BlockSpec(memory_space=pltpu.SMEM)
     anywhere = pl.BlockSpec(memory_space=pl.ANY)
-    width = GROUP * LANES
+    width = max(GROUPS) * LANES
+    packed = [round_up(group * per_device, 16) for group in GROUPS]
     peers = records - 1
-    slot = pltpu.VMEM((records, packed_rows, LANES), jnp.bfloat16)
+    slots = [pltpu.VMEM((records, rows, LANES), jnp.bfloat16) for rows in packed]
     return pl.pallas_call(
-        functools.partial(exchange_kernel, records, per_device, chunks),
+        functools.partial(exchange_kernel, records, per_device, stride),
         out_shape=(
-            jax.ShapeDtypeStruct((per_device * records, chunks * width), jnp.bfloat16),
+            jax.ShapeDtypeStruct((n_rows, GROUPS[-1] * LANES), jnp.bfloat16),
             jax.ShapeDtypeStruct((8, LANES), jnp.float32),
+            jax.ShapeDtypeStruct((n_rows, n_samples), jnp.float32),
         ),
-        in_specs=[anywhere, anywhere, vmem, vmem, vmem, anywhere, smem, smem, vmem, vmem],
-        out_specs=(vmem, vmem),
+        in_specs=[anywhere] * 7 + [smem, smem, vmem, vmem],
+        out_specs=(vmem, vmem, anywhere),
         scratch_shapes=[
             pltpu.VMEM((n_channels, n_samples), jnp.float32),
             pltpu.VMEM((padded, n_samples), jnp.bfloat16),
             pltpu.VMEM(forward.shape, jnp.bfloat16),
+            pltpu.VMEM(wave.shape, jnp.bfloat16),
+            pltpu.VMEM(back.shape, jnp.bfloat16),
+            pltpu.VMEM(vertical.shape, jnp.float32),
             pltpu.VMEM(taps.shape, jnp.float32),
+            pltpu.VMEM((early, n_samples), jnp.bfloat16),
             pltpu.VMEM((records * stride, padded), jnp.bfloat16),
             pltpu.VMEM((padded, width), jnp.bfloat16),
             pltpu.VMEM((padded, width), jnp.bfloat16),
-            pltpu.VMEM((records, packed_rows, LANES), jnp.float32),
-            pltpu.VMEM((records, packed_rows, LANES), jnp.float32),
-            pltpu.VMEM((GROUP, per_device * records, LANES), jnp.float32),
+            pltpu.VMEM((records, max(packed), LANES), jnp.float32),
+            pltpu.VMEM((records, max(packed), LANES), jnp.float32),
+            pltpu.VMEM((max(GROUPS), n_rows, LANES), jnp.float32),
+            pltpu.VMEM((n_rows, early), jnp.bfloat16),
+            pltpu.VMEM((n_rows, n_samples), jnp.float32),
             pltpu.VMEM((records, 8, LANES), jnp.float32),
-            pltpu.SemaphoreType.DMA((1 + 2 * chunks,)),
+            pltpu.SemaphoreType.DMA((16,)),
             pltpu.SemaphoreType.DMA((chunks, peers)),
             pltpu.SemaphoreType.DMA((chunks, peers)),
             pltpu.SemaphoreType.DMA((peers,)),
             pltpu.SemaphoreType.DMA((peers,)),
         ]
-        + [slot] * (2 * chunks),
+        + slots
+        + slots,
         compiler_params=pltpu.CompilerParams(
-            collective_id=0, has_side_effects=True, vmem_limit_bytes=56 * 1024 * 1024
+            collective_id=0, has_side_effects=True, vmem_limit_bytes=58 * 1024 * 1024
         ),
-    )(traces, forward, wave, back, vertical, taps, cable_depth, order, home, channels)
-
-
-def inverse_kernel(count, energy, filtered, inverse, out):
+    )(
+        traces,
+        forward,
+        wave,
+        back,
+        vertical,
+        taps,
+        inverse[:early],
+        cable_depth,
+        shot_slot,
+        gather_home,
+        receiver,
+    )
+
+
+def inverse_kernel(count, energy, partial, filtered, inverse, out):
     total = jnp.sum(energy[...])
     scale = lax.rsqrt(jnp.full((1, 1), 2.0 * FREQ, jnp.float32) * (total / count + energy_eps))
     out[...] = (
-        jnp.dot(filtered[...], inverse[...], preferred_element_type=jnp.float32) * scale
-    )
-
-
-def invert(filtered, energy, inverse, count):
-    n_rows, depth = filtered.shape
-    n_samples = inverse.shape[1]
-    block = 512
+        partial[...] + jnp.dot(filtered[...], inverse[...], preferred_element_type=jnp.float32)
+    ) * scale
+
+
+def invert(partial, filtered, energy, inverse, count):
+    n_rows, n_samples = partial.shape
+    depth = filtered.shape[1]
+    block = max(rows for rows in range(16, 129, 16) if n_rows % rows == 0)
     return pl.pallas_call(
         functools.partial(inverse_kernel, count),
         out_shape=jax.ShapeDtypeStruct((n_rows, n_samples), jnp.float32),
-        grid=(n_samples // block,),
+        grid=(n_rows // block,),
         in_specs=[
             pl.BlockSpec((8, LANES), lambda i: (0, 0)),
-            pl.BlockSpec((n_rows, depth), lambda i: (0, 0)),
-            pl.BlockSpec((depth, block), lambda i: (0, i)),
+            pl.BlockSpec((block, n_samples), lambda i: (i, 0)),
+            pl.BlockSpec((block, depth), lambda i: (i, 0)),
+            pl.BlockSpec((depth, n_samples), lambda i: (0, 0)),
         ],
-        out_specs=pl.BlockSpec((n_rows, block), lambda i: (0, i)),
-        compiler_params=pltpu.CompilerParams(vmem_limit_bytes=48 * 1024 * 1024),
-    )(energy, filtered, inverse)
+        out_specs=pl.BlockSpec((block, n_samples), lambda i: (i, 0)),
+        compiler_params=pltpu.CompilerParams(vmem_limit_bytes=60 * 1024 * 1024),
+    )(energy, partial, filtered, inverse[-depth:])
 
 
 def fused_shards(traces, cable_depth, receiver, shot_slot, gather_home):
@@ -537,10 +630,10 @@
     n_channels, n_samples = traces.shape
     per_device = gather_home.shape[0] // records
     tables = fused_tables(n_channels, n_samples, records, per_device)
-    filtered, energy = exchange(
+    last, energy, partial = exchange(
         traces, cable_depth, receiver, shot_slot, gather_home, tables, records
     )
-    out = invert(filtered, energy, tables[1], float(n_channels * records * FREQ))
+    out = invert(partial, last, energy, tables[1], float(n_channels * records * FREQ))
     return out.reshape(per_device, records, n_samples)
 
 

time: 66.4 us -> 60.4 us (0.910)
  local copies, waits for them, and re-layouts: 3.92 us -> 0 us
  other arithmetic: 2.01 us -> 0 us
    unnamed x4 -> x0, local copies, waits for them, and re-layouts: 2.07 us -> none
    reduce_sum x1 -> x0, other arithmetic: 1.3 us -> none  [exchange(): jnp.sum(jnp.where(shot_slot[None, :] == jnp.arange(records, dtype=jnp.int...]
    broadcast_in_dim x2 -> x0, local copies, waits for them, and re-layouts: 1.17 us -> none  [the longest x1 0.59 us: exchange(): jnp.pad(receiver, (0, padded - n_channels), constant_values=-1)[None, :]]
    add x1 -> x0, other arithmetic: 0.7 us -> none  [exchange(): gather_home // per_device * stride + gather_home % per_device]
    pad x1 -> x0, local copies, waits for them, and re-layouts: 0.69 us -> none  [exchange(): jnp.pad(receiver, (0, padded - n_channels), constant_values=-1)[None, :]]
where the time goes in v1:
time: 60.4 us; the launch traced here: 60.1 us
  Pallas kernels  59.4 us (98%)
  between operations  0.66 us (1%)
    pallas_call x1, Pallas kernels, exchange(): pl.pallas_call(functools.partial(exchange_kernel, records, per_device, st...  51.9 us
    pallas_call x1, Pallas kernels, invert(): pl.pallas_call(functools.partial(inverse_kernel, count), out_shape=jax.Sh...  7.48 us

profile of v1, /device:TPU:0, one launch (start us, length us, event | category | flops | bytes accessed | tf_op | source)
XLA Modules:
  0.0 60.1 jit_solution(626993493381562756)
XLA Ops:
  0.7 51.9 %shard_map.118 = (bf16[672,256]{1,0:T(8,128)(2,1)}, f32[8,128]{1,0:T(8,128)}, f32[672,2048]{1,0:T(8,128)}) custom-call(f32[648,2048]{1,0:T(8,128)} %traces.1, bf16[2048,1152]{1,0:T(8,128)(2,1)} %constant.14.clone.forward, bf16[672,672]{1,0:T(8,128)(2,1)} %constant.15.clone.wave_table, bf16[648,672]{1,0:T(8,128)(2,1)} %constant.16.clone.back_table, ...), custom_call_target="tpu_custom_call" | custom-call | tf_op jit(solution)/shard_map/pallas_call | solution.py:548
  52.6 7.5 %shard_map.119 = f32[672,2048]{1,0:T(8,128)} custom-call(f32[8,128]{1,0:T(8,128)} %get-tuple-element.8.energy, f32[672,2048]{1,0:T(8,128)} %get-tuple-element.9.partial, bf16[672,256]{1,0:T(8,128)(2,1)} %get-tuple-element.10.filtered, bf16[256,2048]{1,0:T(8,128)(2,1)} %constant.20.clone.inverse), custom_call_target="tpu_custom_call" | custom-call | tf_op jit(solution)/shard_map/pallas_call | solution.py:613

commit v2 on v1

--- a/solution.py
+++ b/solution.py
@@ -291,7 +291,7 @@
     receiver,
     last,
     energy,
-    partial,
+    summed,
     raw,
     rounded,
     table,
@@ -307,7 +307,6 @@
     shots,
     ordered,
     filtered,
-    summed,
     sums,
     load_sem,
     send_sem,
@@ -518,13 +517,9 @@
                     part = summed[:, n : n + 512] + part
                 summed[:, n : n + 512] = part
             done = firsts[c + 1]
-        if c == chunks - 2:
-            store = pltpu.make_async_copy(summed, partial, load_sem.at[sem_count[0]])
-            store.start()
     for send in sends[chunks * peers :]:
         send.wait()
     energy[...] = jnp.sum(sums[...], axis=0)
-    store.wait()
 
 
 def exchange(traces, cable_depth, receiver, shot_slot, gather_home, tables, records):
@@ -548,12 +543,12 @@
     return pl.pallas_call(
         functools.partial(exchange_kernel, records, per_device, stride),
         out_shape=(
-            jax.ShapeDtypeStruct((n_rows, GROUPS[-1] * LANES), jnp.bfloat16),
-            jax.ShapeDtypeStruct((8, LANES), jnp.float32),
-            jax.ShapeDtypeStruct((n_rows, n_samples), jnp.float32),
+            pltpu.VMEM((n_rows, GROUPS[-1] * LANES), jnp.bfloat16),
+            pltpu.VMEM((8, LANES), jnp.float32),
+            pltpu.VMEM((n_rows, n_samples), jnp.float32),
         ),
         in_specs=[anywhere] * 7 + [smem, smem, vmem, vmem],
-        out_specs=(vmem, vmem, anywhere),
+        out_specs=(vmem, vmem, vmem),
         scratch_shapes=[
             pltpu.VMEM((n_channels, n_samples), jnp.float32),
             pltpu.VMEM((padded, n_samples), jnp.bfloat16),
@@ -570,7 +565,6 @@
             pltpu.VMEM((records, max(packed), LANES), jnp.float32),
             pltpu.VMEM((max(GROUPS), n_rows, LANES), jnp.float32),
             pltpu.VMEM((n_rows, early), jnp.bfloat16),
-            pltpu.VMEM((n_rows, n_samples), jnp.float32),
             pltpu.VMEM((records, 8, LANES), jnp.float32),
             pltpu.SemaphoreType.DMA((16,)),
             pltpu.SemaphoreType.DMA((chunks, peers)),
@@ -581,7 +575,7 @@
         + slots
         + slots,
         compiler_params=pltpu.CompilerParams(
-            collective_id=0, has_side_effects=True, vmem_limit_bytes=58 * 1024 * 1024
+            collective_id=0, has_side_effects=True, vmem_limit_bytes=54 * 1024 * 1024
         ),
     )(
         traces,
@@ -598,30 +592,40 @@
     )
 
 
-def inverse_kernel(count, energy, partial, filtered, inverse, out):
+def inverse_kernel(count, block, energy, partial, filtered, inverse, out, staged, sems):
     total = jnp.sum(energy[...])
     scale = lax.rsqrt(jnp.full((1, 1), 2.0 * FREQ, jnp.float32) * (total / count + energy_eps))
-    out[...] = (
-        partial[...] + jnp.dot(filtered[...], inverse[...], preferred_element_type=jnp.float32)
-    ) * scale
+    stores = []
+    for i, row in enumerate(range(0, partial.shape[0], block)):
+        rows = slice(row, row + block)
+        staged[rows, :] = (
+            partial[rows, :]
+            + jnp.dot(filtered[rows, :], inverse[...], preferred_element_type=jnp.float32)
+        ) * scale
+        store = pltpu.make_async_copy(
+            staged.at[pl.ds(row, block), :], out.at[pl.ds(row, block), :], sems.at[i]
+        )
+        store.start()
+        stores.append(store)
+    for store in stores:
+        store.wait()
 
 
 def invert(partial, filtered, energy, inverse, count):
     n_rows, n_samples = partial.shape
     depth = filtered.shape[1]
     block = max(rows for rows in range(16, 129, 16) if n_rows % rows == 0)
+    vmem = pl.BlockSpec(memory_space=pltpu.VMEM)
     return pl.pallas_call(
-        functools.partial(inverse_kernel, count),
+        functools.partial(inverse_kernel, count, block),
         out_shape=jax.ShapeDtypeStruct((n_rows, n_samples), jnp.float32),
-        grid=(n_rows // block,),
-        in_specs=[
-            pl.BlockSpec((8, LANES), lambda i: (0, 0)),
-            pl.BlockSpec((block, n_samples), lambda i: (i, 0)),
-            pl.BlockSpec((block, depth), lambda i: (i, 0)),
-            pl.BlockSpec((depth, n_samples), lambda i: (0, 0)),
+        in_specs=[vmem] * 4,
+        out_specs=pl.BlockSpec(memory_space=pl.ANY),
+        scratch_shapes=[
+            pltpu.VMEM((n_rows, n_samples), jnp.float32),
+            pltpu.SemaphoreType.DMA((n_rows // block,)),
         ],
-        out_specs=pl.BlockSpec((block, n_samples), lambda i: (i, 0)),
-        compiler_params=pltpu.CompilerParams(vmem_limit_bytes=60 * 1024 * 1024),
+        compiler_params=pltpu.CompilerParams(vmem_limit_bytes=40 * 1024 * 1024),
     )(energy, partial, filtered, inverse[-depth:])
 
 

time: 60.4 us -> 55.1 us (0.912)
  Pallas kernels: 59.4 us -> 54.1 us
    pallas_call x1, Pallas kernels: 7.48 us -> 2.82 us  [invert(): pl.pallas_call(functools.partial(inverse_kernel, count, block), out_shape...]
    pallas_call x1, Pallas kernels: 51.9 us -> 51.3 us  [exchange(): pl.pallas_call(functools.partial(exchange_kernel, records, per_device, st...]
where the time goes in v2:
time: 55.1 us; the launch traced here: 54.9 us
  Pallas kernels  54.1 us (98%)
  between operations  0.84 us (2%)
    pallas_call x1, Pallas kernels, exchange(): pl.pallas_call(functools.partial(exchange_kernel, records, per_device, st...  51.3 us
    pallas_call x1, Pallas kernels, invert(): pl.pallas_call(functools.partial(inverse_kernel, count, block), out_shape...  2.82 us

profile of v2, /device:TPU:0, one launch (start us, length us, event | category | flops | bytes accessed | tf_op | source)
XLA Modules:
  0.0 54.9 jit_solution(12486984548624623481)
XLA Ops:
  0.7 0.0 copy-start
  0.7 51.3 %shard_map.118 = (bf16[672,256]{1,0:T(8,128)(2,1)S(1)}, f32[8,128]{1,0:T(8,128)S(1)}, f32[672,2048]{1,0:T(8,128)S(1)}) custom-call(f32[648,2048]{1,0:T(8,128)} %traces.1, bf16[2048,1152]{1,0:T(8,128)(2,1)} %constant.14.clone.forward, bf16[672,672]{1,0:T(8,128)(2,1)} %constant.15.clone.wave_table, bf16[648,672]{1,0:T(8,128)(2,1)} %constant.16.clone.back_table, ...), custom_call_target="tpu_custom_call" | custom-call | tf_op jit(solution)/shard_map/pallas_call | solution.py:543
  51.9 0.0 copy-done
  52.0 2.8 %shard_map.119 = f32[672,2048]{1,0:T(8,128)} custom-call(f32[8,128]{1,0:T(8,128)S(1)} %get-tuple-element.8.energy, f32[672,2048]{1,0:T(8,128)S(1)} %get-tuple-element.9.partial, bf16[672,256]{1,0:T(8,128)(2,1)S(1)} %get-tuple-element.10.filtered, bf16[256,2048]{1,0:T(8,128)(2,1)S(1)} %copy-done), custom_call_target="tpu_custom_call" | custom-call | tf_op jit(solution)/shard_map/pallas_call | solution.py:619
Async XLA Ops:
  0.7 51.3 %copy-start = (bf16[256,2048]{1,0:T(8,128)(2,1)S(1)}, bf16[256,2048]{1,0:T(8,128)(2,1)}, u32[]{:S(2)}) copy-start(bf16[256,2048]{1,0:T(8,128)(2,1)} %constant.20.clone.inverse) | copy-start | bytes 3145732

commit v3 on v2

--- a/solution.py
+++ b/solution.py
@@ -183,7 +183,12 @@
 
 LANES = 128
 HALF = LANES // 2
-GROUPS = (1, 3, 3, 2)
+GROUPS = (2, 2, 2, 2, 1)
+
+
+def band_rows(per_device):
+    ends = [sum(GROUPS[: c + 1]) * per_device for c in range(len(GROUPS))]
+    return [0] + [end // 16 * 16 for end in ends[:-1]] + [round_up(ends[-1], 16)]
 
 
 def fused_tables(n_channels, n_samples, records, per_device):
@@ -233,15 +238,8 @@
     lag = lag.reshape(records, blocks, 1, HALF)
     lag = np.concatenate([lag, lag], axis=2).reshape(records, blocks, 1, LANES)
     lag = np.broadcast_to(lag, (records, blocks, per_device, LANES))
-    taps = []
-    first = 0
-    for group in GROUPS:
-        filled = group * per_device
-        part = np.zeros((records, round_up(filled, 16), LANES))
-        part[:, :filled] = lag[:, first : first + group].reshape(records, filled, LANES)
-        taps.append(part)
-        first += group
-    taps = np.concatenate(taps, axis=1)
+    taps = np.zeros((records, band_rows(per_device)[-1], LANES))
+    taps[:, : blocks * per_device] = lag.reshape(records, blocks * per_device, LANES)
     return (
         forward.astype(bf16),
         inverse.astype(bf16),
@@ -324,8 +322,8 @@
     home_rows = placed.shape[0]
     peers = records - 1
     firsts = [sum(GROUPS[:c]) for c in range(chunks + 1)]
-    packed_rows = [ref.shape[1] for ref in outgoing]
-    tap_rows = [sum(packed_rows[:c]) for c in range(chunks)]
+    bounds = band_rows(per_device)
+    finished = [bound // per_device for bound in bounds[:-1]] + [firsts[-1]]
 
     start = (lax.rem(me // 4, 2) * 2 + lax.rem(me, 2)) * peers // 4
 
@@ -354,15 +352,19 @@
         lanes = pl.ds(firsts[c] * LANES, GROUPS[c] * LANES)
         return load(forward.at[:, lanes], table.at[:, lanes])
 
-    piece = round_up(-(-n_channels // 3), 16)
+    piece = round_up(-(-padded // 3), 16)
     back_load = load(back_table, back)
+    column_loads = [load_columns(0)]
     pieces = []
-    for row in range(0, n_channels, piece):
-        rows = pl.ds(row, min(piece, n_channels - row))
-        pieces.append((row, load(traces.at[rows, :], raw.at[rows, :])))
-    column_loads = [load_columns(0)]
+    for row in range(0, padded, piece):
+        end = min(row + piece, n_channels)
+        middle = row + round_up((end - row) // 2, 8)
+        halves = [pl.ds(row, middle - row), pl.ds(middle, end - middle)]
+        pieces.append((row, end, [load(traces.at[rows, :], raw.at[rows, :]) for rows in halves]))
     wave_load = load(wave_table, wave)
-    vertical_load = load(vertical_table, vertical)
+    near = pl.ds(0, firsts[1] * LANES)
+    far = pl.ds(firsts[1] * LANES, (firsts[-1] - firsts[1]) * LANES)
+    vertical_load = load(vertical_table.at[:, near], vertical.at[:, near])
 
     barrier = pltpu.get_barrier_semaphore()
     for step in range(1, records):
@@ -388,36 +390,50 @@
     chosen = (rows == moved).astype(jnp.bfloat16)
     placed[...] = jnp.dot(chosen, by_bin, preferred_element_type=jnp.float32).astype(jnp.bfloat16)
 
-    for row, copy in pieces:
-        copy.wait()
-        end = min(row + piece, n_channels)
+    def gains(c):
+        return [
+            gain_tiles(vertical[:, j * LANES : (j + 1) * LANES], depth[0], n_channels)
+            for j in range(firsts[c], firsts[c + 1])
+        ]
+
+    vertical_load.wait()
+    band_gains = gains(0)
+    column_loads[0].wait()
+    for row, end, copies in pieces:
+        for copy in copies:
+            copy.wait()
         rounded[row:end, :] = raw[row:end, :].astype(jnp.bfloat16)
+        full = min(row + piece, padded)
+        spectra[row:full, : GROUPS[0] * LANES] = jnp.dot(
+            rounded[row:full, :],
+            table[:, : GROUPS[0] * LANES],
+            preferred_element_type=jnp.float32,
+        ).astype(jnp.bfloat16)
     column_loads += [load_columns(c) for c in range(1, chunks)]
+    far_load = load(vertical_table.at[:, far], vertical.at[:, far])
     lag_load = load(taps, lag)
     inverse_load = load(inverse_table, inverse)
 
     total = jnp.zeros((8, LANES), jnp.float32)
     sends = []
     for c, group in enumerate(GROUPS):
-        column_loads[c].wait()
-        spectra[:, : group * LANES] = jnp.dot(
-            rounded[...],
-            table[:, firsts[c] * LANES : firsts[c + 1] * LANES],
-            preferred_element_type=jnp.float32,
-        ).astype(jnp.bfloat16)
         if c == 0:
             wave_load.wait()
+        else:
+            column_loads[c].wait()
+            if c == 1:
+                far_load.wait()
+            band_gains = gains(c)
+            spectra[:, : group * LANES] = jnp.dot(
+                rounded[...],
+                table[:, firsts[c] * LANES : firsts[c + 1] * LANES],
+                preferred_element_type=jnp.float32,
+            ).astype(jnp.bfloat16)
         turned = jnp.dot(
             wave[...], spectra[:, : group * LANES], preferred_element_type=jnp.float32
         )
-        if c == 0:
-            vertical_load.wait()
-        for b in range(group):
+        for b, (straight, crossed) in enumerate(band_gains):
             lanes = slice(b * LANES, (b + 1) * LANES)
-            column = firsts[c] + b
-            straight, crossed = gain_tiles(
-                vertical[:, column * LANES : (column + 1) * LANES], depth[0], n_channels
-            )
             for part in range(2):
                 part_rows = slice(part * half_rows, (part + 1) * half_rows)
                 value = turned[part_rows, lanes]
@@ -430,11 +446,12 @@
         for b in range(group):
             block = cleaned[:, b * LANES : (b + 1) * LANES]
             total = total + jnp.sum((block * block).reshape(-1, 8, LANES), axis=0)
+            first = (firsts[c] + b) * per_device
             for d in range(records):
-                packed[d, b * per_device : (b + 1) * per_device, :] = block[
+                packed[d, first : first + per_device, :] = block[
                     d * stride : d * stride + per_device
                 ]
-        outgoing[c][...] = packed[:, : packed_rows[c], :].astype(jnp.bfloat16)
+        outgoing[c][...] = packed[:, bounds[c] : bounds[c + 1], :].astype(jnp.bfloat16)
         if c == 0:
             pl.semaphore_wait(barrier, peers)
         for i in range(peers):
@@ -482,31 +499,29 @@
 
         def filter_rows(r, carry):
             at = pl.ds(pl.multiple_of(r * tile, tile), tile)
-            tap_at = pl.ds(pl.multiple_of(tap_rows[c] + r * tile, tile), tile)
+            tap_at = pl.ds(pl.multiple_of(bounds[c] + r * tile, tile), tile)
             values = [arrived[c][order[q], at, :].astype(jnp.float32) for q in range(records)]
             for p in range(records):
                 result = None
                 for q in range(records):
                     term = lag[abs(p - q), tap_at, :] * values[q]
                     result = term if result is None else result + term
-                shots[p, at, :] = result
+                shots[p, tap_at, :] = result
             return carry
 
-        lax.fori_loop(0, packed_rows[c] // tile, filter_rows, 0)
-        for b in range(group):
+        lax.fori_loop(0, (bounds[c + 1] - bounds[c]) // tile, filter_rows, 0)
+        for j in range(finished[c], finished[c + 1]):
             for p in range(records):
-                ordered[b, pl.ds(p, per_device, stride=records), :] = shots[
-                    p, b * per_device : (b + 1) * per_device, :
+                ordered[j, pl.ds(p, per_device, stride=records), :] = shots[
+                    p, j * per_device : (j + 1) * per_device, :
                 ]
             if c == chunks - 1:
-                last[:, b * LANES : (b + 1) * LANES] = ordered[b].astype(jnp.bfloat16)
+                b = j - finished[c]
+                last[:, b * LANES : (b + 1) * LANES] = ordered[j].astype(jnp.bfloat16)
             else:
-                column = firsts[c] + b
-                filtered[:, column * LANES : (column + 1) * LANES] = ordered[b].astype(
-                    jnp.bfloat16
-                )
+                filtered[:, j * LANES : (j + 1) * LANES] = ordered[j].astype(jnp.bfloat16)
         if 0 < c < chunks - 1:
-            depth_at = slice(done * LANES, firsts[c + 1] * LANES)
+            depth_at = slice(done * LANES, finished[c + 1] * LANES)
             for n in range(0, n_samples, 512):
                 part = jnp.dot(
                     filtered[:, depth_at],
@@ -516,7 +531,7 @@
                 if done:
                     part = summed[:, n : n + 512] + part
                 summed[:, n : n + 512] = part
-            done = firsts[c + 1]
+            done = finished[c + 1]
     for send in sends[chunks * peers :]:
         send.wait()
     energy[...] = jnp.sum(sums[...], axis=0)
@@ -532,18 +547,20 @@
     padded = wave.shape[0]
     n_rows = per_device * records
     chunks = len(GROUPS)
-    early = sum(GROUPS[:-1]) * LANES
+    bounds = band_rows(per_device)
+    late = sum(GROUPS) - bounds[-2] // per_device
+    early = (sum(GROUPS) - late) * LANES
     vmem = pl.BlockSpec(memory_space=pltpu.VMEM)
     smem = pl.BlockSpec(memory_space=pltpu.SMEM)
     anywhere = pl.BlockSpec(memory_space=pl.ANY)
     width = max(GROUPS) * LANES
-    packed = [round_up(group * per_device, 16) for group in GROUPS]
+    packed = [bounds[c + 1] - bounds[c] for c in range(chunks)]
     peers = records - 1
     slots = [pltpu.VMEM((records, rows, LANES), jnp.bfloat16) for rows in packed]
     return pl.pallas_call(
         functools.partial(exchange_kernel, records, per_device, stride),
         out_shape=(
-            pltpu.VMEM((n_rows, GROUPS[-1] * LANES), jnp.bfloat16),
+            pltpu.VMEM((n_rows, late * LANES), jnp.bfloat16),
             pltpu.VMEM((8, LANES), jnp.float32),
             pltpu.VMEM((n_rows, n_samples), jnp.float32),
         ),
@@ -561,12 +578,12 @@
             pltpu.VMEM((records * stride, padded), jnp.bfloat16),
             pltpu.VMEM((padded, width), jnp.bfloat16),
             pltpu.VMEM((padded, width), jnp.bfloat16),
-            pltpu.VMEM((records, max(packed), LANES), jnp.float32),
-            pltpu.VMEM((records, max(packed), LANES), jnp.float32),
-            pltpu.VMEM((max(GROUPS), n_rows, LANES), jnp.float32),
+            pltpu.VMEM((records, bounds[-1], LANES), jnp.float32),
+            pltpu.VMEM((records, bounds[-1], LANES), jnp.float32),
+            pltpu.VMEM((sum(GROUPS), n_rows, LANES), jnp.float32),
             pltpu.VMEM((n_rows, early), jnp.bfloat16),
             pltpu.VMEM((records, 8, LANES), jnp.float32),
-            pltpu.SemaphoreType.DMA((16,)),
+            pltpu.SemaphoreType.DMA((24,)),
             pltpu.SemaphoreType.DMA((chunks, peers)),
             pltpu.SemaphoreType.DMA((chunks, peers)),
             pltpu.SemaphoreType.DMA((peers,)),

time: 55.1 us -> 55.1 us (level)
  no operation moved by 1% of the time
where the time goes in v3:
time: 55.1 us; the launch traced here: 54.9 us
  Pallas kernels  54.1 us (98%)
  between operations  0.84 us (2%)
    pallas_call x1, Pallas kernels, exchange(): pl.pallas_call(functools.partial(exchange_kernel, records, per_device, st...  51.3 us
    pallas_call x1, Pallas kernels, invert(): pl.pallas_call(functools.partial(inverse_kernel, count, block), out_shape...  2.78 us

profile of v3, /device:TPU:0, one launch (start us, length us, event | category | flops | bytes accessed | tf_op | source)
XLA Modules:
  0.0 54.9 jit_solution(695581633209821148)
XLA Ops:
  0.7 0.0 copy-start
  0.7 51.3 %shard_map.118 = (bf16[672,128]{1,0:T(8,128)(2,1)S(1)}, f32[8,128]{1,0:T(8,128)S(1)}, f32[672,2048]{1,0:T(8,128)S(1)}) custom-call(f32[648,2048]{1,0:T(8,128)} %traces.1, bf16[2048,1152]{1,0:T(8,128)(2,1)} %constant.14.clone.forward, bf16[672,672]{1,0:T(8,128)(2,1)} %constant.15.clone.wave_table, bf16[648,672]{1,0:T(8,128)(2,1)} %constant.16.clone.back_table, ...), custom_call_target="tpu_custom_call" | custom-call | tf_op jit(solution)/shard_map/pallas_call | solution.py:560
  51.9 0.0 copy-done
  52.0 2.8 %shard_map.119 = f32[672,2048]{1,0:T(8,128)} custom-call(f32[8,128]{1,0:T(8,128)S(1)} %get-tuple-element.8.energy, f32[672,2048]{1,0:T(8,128)S(1)} %get-tuple-element.9.partial, bf16[672,128]{1,0:T(8,128)(2,1)S(1)} %get-tuple-element.10.filtered, bf16[128,2048]{1,0:T(8,128)(2,1)S(1)} %copy-done), custom_call_target="tpu_custom_call" | custom-call | tf_op jit(solution)/shard_map/pallas_call | solution.py:636
Async XLA Ops:
  0.7 51.3 %copy-start = (bf16[128,2048]{1,0:T(8,128)(2,1)S(1)}, bf16[128,2048]{1,0:T(8,128)(2,1)}, u32[]{:S(2)}) copy-start(bf16[128,2048]{1,0:T(8,128)(2,1)} %constant.20.clone.inverse) | copy-start | bytes 1572868

commit v4 on v3

--- a/solution.py
+++ b/solution.py
@@ -499,14 +499,16 @@
 
         def filter_rows(r, carry):
             at = pl.ds(pl.multiple_of(r * tile, tile), tile)
-            tap_at = pl.ds(pl.multiple_of(bounds[c] + r * tile, tile), tile)
             values = [arrived[c][order[q], at, :].astype(jnp.float32) for q in range(records)]
-            for p in range(records):
-                result = None
-                for q in range(records):
-                    term = lag[abs(p - q), tap_at, :] * values[q]
-                    result = term if result is None else result + term
-                shots[p, tap_at, :] = result
+            for low in range(0, tile, 8):
+                tap_at = pl.ds(pl.multiple_of(bounds[c] + r * tile + low, 8), 8)
+                band_taps = [lag[apart, tap_at, :] for apart in range(records)]
+                parts = [value[low : low + 8] for value in values]
+                for p in range(records):
+                    result = band_taps[p] * parts[0]
+                    for q in range(1, records):
+                        result = result + band_taps[abs(p - q)] * parts[q]
+                    shots[p, tap_at, :] = result
             return carry
 
         lax.fori_loop(0, (bounds[c + 1] - bounds[c]) // tile, filter_rows, 0)

time: 55.1 us -> 54.9 us (level)
  no operation moved by 1% of the time
where the time goes in v4:
time: 54.9 us; the launch traced here: 54.7 us
  Pallas kernels  53.9 us (98%)
  between operations  0.84 us (2%)
    pallas_call x1, Pallas kernels, exchange(): pl.pallas_call(functools.partial(exchange_kernel, records, per_device, st...  51.1 us
    pallas_call x1, Pallas kernels, invert(): pl.pallas_call(functools.partial(inverse_kernel, count, block), out_shape...  2.78 us

profile of v4, /device:TPU:0, one launch (start us, length us, event | category | flops | bytes accessed | tf_op | source)
XLA Modules:
  0.0 54.7 jit_solution(16382448442722968242)
XLA Ops:
  0.7 0.0 copy-start
  0.7 51.1 %shard_map.118 = (bf16[672,128]{1,0:T(8,128)(2,1)S(1)}, f32[8,128]{1,0:T(8,128)S(1)}, f32[672,2048]{1,0:T(8,128)S(1)}) custom-call(f32[648,2048]{1,0:T(8,128)} %traces.1, bf16[2048,1152]{1,0:T(8,128)(2,1)} %constant.14.clone.forward, bf16[672,672]{1,0:T(8,128)(2,1)} %constant.15.clone.wave_table, bf16[648,672]{1,0:T(8,128)(2,1)} %constant.16.clone.back_table, ...), custom_call_target="tpu_custom_call" | custom-call | tf_op jit(solution)/shard_map/pallas_call | solution.py:562
  51.8 0.0 copy-done
  51.8 2.8 %shard_map.119 = f32[672,2048]{1,0:T(8,128)} custom-call(f32[8,128]{1,0:T(8,128)S(1)} %get-tuple-element.8.energy, f32[672,2048]{1,0:T(8,128)S(1)} %get-tuple-element.9.partial, bf16[672,128]{1,0:T(8,128)(2,1)S(1)} %get-tuple-element.10.filtered, bf16[128,2048]{1,0:T(8,128)(2,1)S(1)} %copy-done), custom_call_target="tpu_custom_call" | custom-call | tf_op jit(solution)/shard_map/pallas_call | solution.py:638
Async XLA Ops:
  0.7 51.1 %copy-start = (bf16[128,2048]{1,0:T(8,128)(2,1)S(1)}, bf16[128,2048]{1,0:T(8,128)(2,1)}, u32[]{:S(2)}) copy-start(bf16[128,2048]{1,0:T(8,128)(2,1)} %constant.20.clone.inverse) | copy-start | bytes 1572868
